TPU v7x, 32 devices: a whole 2x2x4 slice. The times are simulated.
32 devices in a mesh: tok: 8 (over z, x), ad: 4 (over y, core).
Axes of the slice: x: 2, y: 2, z: 4, core: 2. Of those that a mesh axis runs over, the one named last changes fastest.
Arguments:
- tokens: bfloat16 [8192, 768], P('tok'), may hold values from -6 to 6
- cotangent: bfloat16 [8192, 768], P('tok'), may hold values from -6 to 6
- attn_qkv: bfloat16 [3, 768, 768], P(None, None, 'ad'), may hold values from -0.21875 to 0.21875
- attn_out: bfloat16 [768, 768], P('ad'), may hold values from -4 to 4
- ffn_in: bfloat16 [768, 3072], P(None, 'ad'), may hold values from -0.21875 to 0.21875
- ffn_bias_in: float32 [3072], P('ad'), may hold values from -1.5 to 1.5
- ffn_out: bfloat16 [3072, 768], P('ad'), may hold values from -0.109375 to 0.109375
- ffn_bias_out: float32 [768], replicated, may hold values from -1.5 to 1.5
- norm_gains: float32 [3, 768], replicated, may hold values from 0.5 to 1.5
- norm_shifts: float32 [3, 768], replicated, may hold values from -1.5 to 1.5
- adapter_down: bfloat16 [768, 768], P(None, 'ad'), may hold values from -0.21875 to 0.21875
- adapter_up: bfloat16 [16, 48, 768], P('ad'), may hold values from -0.875 to 0.875
- merging_proj: bfloat16 [3, 768, 768], replicated, may hold values from -0.21875 to 0.21875
- adapter_mask: int32 [8, 16], P('tok', 'ad'), may hold values from 0 to 1, as said below
- lengths: int32 [8], P('tok'), may hold values from 256 to 1024, as said below
Outputs:
- output: bfloat16 [8192, 768], P('tok')
- grad_tokens: float32 [8192, 768], P('tok')
- grad_attn_qkv: float32 [3, 768, 768], P(None, None, 'ad')
- grad_attn_out: float32 [768, 768], P('ad')
- grad_ffn_in: float32 [768, 3072], P(None, 'ad')
- grad_ffn_bias_in: float32 [3072], P('ad')
- grad_ffn_out: float32 [3072, 768], P('ad')
- grad_ffn_bias_out: float32 [768], replicated
- grad_norm_gains: float32 [3, 768], replicated
- grad_norm_shifts: float32 [3, 768], replicated
- grad_merging: float32 [3, 768, 768], replicated
- usage: float32 [16], P('ad')
Inputs may be any that keep to these rules, and one draw needn't show every extreme that they name: `adapter_mask`: every sequence has at least one available adapter. `lengths`: one sequence, drawn from the seed, has exactly 1024 tokens; positions at or past a sequence's length are padding.
All inputs are finite; a program needn't handle non-finite values.
Results may differ from a plain program's by a relative error of at most 0.03.
Values may be sent and summed in bfloat16 or wider, within the bound.
No kernel may reach another device: no remote copies, remote signals or barrier semaphores. Data moves between devices by JAX's collectives and lax.ppermute only.
A program may use at most 192 MiB of HBM per device.

v0:
```python
import jax
import jax.numpy as jnp
from jax import lax
from jax.sharding import PartitionSpec as P

HEAD = 64


HIGHEST = lax.Precision.HIGHEST
EPSILON = 1e-06
NEGATIVE = -1e30
BLOCK_LIMIT = 512


def normalize(values, gain, shift):
    centred = values - jnp.mean(values, -1, keepdims=True)
    inverse = lax.rsqrt(jnp.mean(centred * centred, -1, keepdims=True) + EPSILON)
    unit_rows = centred * inverse
    return (unit_rows * gain + shift, unit_rows, inverse)


def normalize_back(gradient, unit_rows, inverse, gain):
    scaled = gradient * gain
    centred = (
        scaled
        - jnp.mean(scaled, -1, keepdims=True)
        - unit_rows * jnp.mean(scaled * unit_rows, -1, keepdims=True)
    )
    return (centred * inverse, jnp.sum(gradient * unit_rows, 0), jnp.sum(gradient, 0))


def gelu_exact(values):
    return jax.nn.gelu(values, approximate=False)


def gelu_back(values, gradient):
    return jax.vjp(gelu_exact, values)[1](gradient)[0]


def split_packed(packed):
    positions = packed.shape[1]
    heads = packed.shape[2] // HEAD
    block_rows = min(BLOCK_LIMIT, positions)
    key_rows = packed[1].reshape(positions, heads, HEAD)
    value_rows = packed[2].reshape(positions, heads, HEAD)
    queries = packed[0].reshape(positions // block_rows, block_rows, heads, HEAD)
    return (queries, key_rows, value_rows, block_rows)


def attend(arguments):
    packed, keep = arguments
    queries, key_rows, value_rows, block_rows = split_packed(packed)
    scaling = HEAD ** (-0.5)

    def one_block(query_rows):
        logits = (
            jnp.einsum("qhd,khd->hqk", query_rows, key_rows, preferred_element_type=jnp.float32)
            * scaling
        )
        logits = jnp.where(keep[None, None, :], logits, NEGATIVE)
        highest = jnp.max(logits, -1, keepdims=True)
        expon = jnp.exp(logits - highest)
        totals = jnp.sum(expon, -1, keepdims=True)
        weights = (expon / totals).astype(jnp.bfloat16)
        context = jnp.einsum(
            "hqk,khd->qhd", weights, value_rows, preferred_element_type=jnp.float32
        )
        return (
            context.astype(jnp.bfloat16).reshape(block_rows, -1),
            (highest + jnp.log(totals))[:, :, 0],
        )

    context, log_totals = lax.map(one_block, queries)
    return (context.reshape(packed.shape[1], -1), log_totals)


def attend_back(arguments):
    packed, log_totals, grad_context, keep = arguments
    queries, key_rows, value_rows, block_rows = split_packed(packed)
    scaling = HEAD ** (-0.5)
    gradients = grad_context.reshape(queries.shape)

    def one_block(carried, pieces):
        query_rows, log_block, grad_block = pieces
        logits = (
            jnp.einsum("qhd,khd->hqk", query_rows, key_rows, preferred_element_type=jnp.float32)
            * scaling
        )
        logits = jnp.where(keep[None, None, :], logits, NEGATIVE)
        probs = jnp.exp(logits - log_block[:, :, None])
        grad_probs = jnp.einsum(
            "qhd,khd->hqk", grad_block, value_rows, preferred_element_type=jnp.float32
        )
        inner_sum = jnp.sum(probs * grad_probs, -1, keepdims=True)
        grad_logits = (probs * (grad_probs - inner_sum)).astype(jnp.bfloat16)
        grad_query = (
            jnp.einsum("hqk,khd->qhd", grad_logits, key_rows, preferred_element_type=jnp.float32)
            * scaling
        )
        grad_keys = (
            carried[0]
            + jnp.einsum(
                "hqk,qhd->khd", grad_logits, query_rows, preferred_element_type=jnp.float32
            )
            * scaling
        )
        grad_values = carried[1] + jnp.einsum(
            "hqk,qhd->khd",
            probs.astype(jnp.bfloat16),
            grad_block,
            preferred_element_type=jnp.float32,
        )
        return ((grad_keys, grad_values), grad_query)

    zero_rows = jnp.zeros(key_rows.shape, jnp.float32)
    (grad_keys, grad_values), grad_query = lax.scan(
        one_block, (zero_rows, zero_rows), (queries, log_totals, gradients)
    )
    positions = packed.shape[1]
    return jnp.stack(
        [
            grad_query.reshape(positions, -1),
            grad_keys.reshape(positions, -1),
            grad_values.reshape(positions, -1),
        ]
    ).astype(jnp.bfloat16)


def on_device(
    tokens,
    cotangent,
    attn_qkv,
    attn_out,
    ffn_in,
    ffn_bias_in,
    ffn_out,
    ffn_bias_out,
    norm_gains,
    norm_shifts,
    adapter_down,
    adapter_up,
    merging_proj,
    adapter_mask,
    lengths,
):
    sequences = lengths.shape[0]
    row_count = tokens.shape[0]
    positions = row_count // sequences
    model_width = tokens.shape[1]
    keep = jnp.arange(positions)[None, :] < lengths[:, None]
    seq_tokens = tokens.reshape(sequences, positions, model_width)
    packed = jnp.einsum(
        "std,jde->sjte", seq_tokens, attn_qkv, preferred_element_type=jnp.float32
    ).astype(jnp.bfloat16)
    context, log_totals = lax.map(attend, (packed, keep))
    context = context.reshape(row_count, -1)
    attended = lax.psum(
        jnp.dot(context, attn_out, preferred_element_type=jnp.float32).astype(jnp.bfloat16), "ad"
    ).astype(jnp.float32)
    first, unit_first, inverse_first = normalize(
        tokens.astype(jnp.float32) + attended, norm_gains[0], norm_shifts[0]
    )
    first_low = first.astype(jnp.bfloat16)
    inner_pre = jnp.dot(first_low, ffn_in, preferred_element_type=jnp.float32) + ffn_bias_in
    inner = gelu_exact(inner_pre).astype(jnp.bfloat16)
    fed_rows = (
        lax.psum(jnp.dot(inner, ffn_out, preferred_element_type=jnp.float32), "ad") + ffn_bias_out
    )
    down_whole, up_whole = (adapter_down, adapter_up)
    mask_rows = adapter_mask.astype(jnp.float32)
    row_ids = jnp.arange(row_count)
    held_adapters = up_whole.shape[0]
    owner = (row_ids[:, None] // positions == jnp.arange(sequences)[None, :]).astype(jnp.float32)
    usable = jnp.dot(owner, mask_rows, precision=HIGHEST) > 0.5
    row_lengths = jnp.dot(owner, lengths.astype(jnp.float32), precision=HIGHEST)
    valid = ((row_ids % positions).astype(jnp.float32) < row_lengths).astype(jnp.float32)
    second, unit_second, inverse_second = normalize(first + fed_rows, norm_gains[1], norm_shifts[1])
    second_low = second.astype(jnp.bfloat16)
    bottle_pre = jnp.dot(second_low, down_whole, preferred_element_type=jnp.float32)
    squeezed = gelu_exact(bottle_pre).astype(jnp.bfloat16).reshape(row_count, held_adapters, -1)
    adapted = (
        second[:, None, :]
        + jnp.einsum("tar,ard->tad", squeezed, up_whole, preferred_element_type=jnp.float32)
    ).astype(jnp.bfloat16)
    fquery = jnp.dot(second_low, merging_proj[0], preferred_element_type=jnp.float32).astype(
        jnp.bfloat16
    )
    fkeys = jnp.einsum(
        "tad,de->tae", adapted, merging_proj[1], preferred_element_type=jnp.float32
    ).astype(jnp.bfloat16)
    fvalues = jnp.einsum(
        "tad,de->tae", adapted, merging_proj[2], preferred_element_type=jnp.float32
    )
    scaling = model_width ** (-0.5)
    scores = jnp.einsum("td,tad->ta", fquery, fkeys, preferred_element_type=jnp.float32) * scaling
    scores = jnp.where(usable, scores, NEGATIVE)
    local_top = jnp.max(scores, -1)
    highest = lax.pmax(local_top, "ad")
    weights = jnp.where(usable, jnp.exp(scores - highest[:, None]), 0.0)
    local_mix = jnp.einsum("ta,tad->td", weights, fvalues, precision=HIGHEST)
    totals, mixed = (
        lax.psum(jnp.sum(weights, -1).astype(jnp.bfloat16), "ad").astype(jnp.float32),
        lax.psum(local_mix.astype(jnp.bfloat16), "ad").astype(jnp.float32),
    )
    probs = weights / totals[:, None]
    blended = mixed / totals[:, None]
    final, unit_third, inverse_third = normalize(second + blended, norm_gains[2], norm_shifts[2])
    output = final.astype(jnp.bfloat16)
    mass = jnp.einsum("ta,t->a", probs, valid, precision=HIGHEST)
    counted = jnp.sum(lengths.astype(jnp.float32))
    cot_rows = cotangent.astype(jnp.float32)
    dthird, gain_third, shift_third = normalize_back(
        cot_rows, unit_third, inverse_third, norm_gains[2]
    )
    dfvalues = (probs[:, :, None] * dthird[:, None, :]).astype(jnp.bfloat16)
    dprobs = jnp.einsum("td,tad->ta", dthird, fvalues, precision=HIGHEST)
    inner_blend = jnp.sum(dthird * blended, -1, keepdims=True)
    dscaled = probs * (dprobs - inner_blend) * scaling
    dfkeys = (dscaled[:, :, None] * fquery.astype(jnp.float32)[:, None, :]).astype(jnp.bfloat16)
    dquery_part = jnp.einsum("ta,tad->td", dscaled, fkeys, precision=HIGHEST)
    dadapted = (
        jnp.einsum("tae,de->tad", dfkeys, merging_proj[1], preferred_element_type=jnp.float32)
        + jnp.einsum("tae,de->tad", dfvalues, merging_proj[2], preferred_element_type=jnp.float32)
    ).astype(jnp.bfloat16)
    grad_fkeys = jnp.einsum("tad,tae->de", adapted, dfkeys, preferred_element_type=jnp.float32)
    grad_fvalues = jnp.einsum("tad,tae->de", adapted, dfvalues, preferred_element_type=jnp.float32)
    group_keys, group_values = (
        lax.psum(grad_fkeys.astype(jnp.bfloat16), "ad").astype(jnp.float32),
        lax.psum(grad_fvalues.astype(jnp.bfloat16), "ad").astype(jnp.float32),
    )
    dsqueezed = jnp.einsum(
        "tad,ard->tar", dadapted, up_whole, preferred_element_type=jnp.float32
    ).reshape(row_count, -1)
    dbottle = gelu_back(bottle_pre, dsqueezed).astype(jnp.bfloat16)
    dsecond_part = jnp.einsum(
        "tc,dc->td", dbottle, down_whole, preferred_element_type=jnp.float32
    ) + jnp.sum(dadapted.astype(jnp.float32), 1)
    dquery, dsecond_sum = (
        lax.psum(dquery_part.astype(jnp.bfloat16), "ad").astype(jnp.float32),
        lax.psum(dsecond_part.astype(jnp.bfloat16), "ad").astype(jnp.float32),
    )
    dquery_low = dquery.astype(jnp.bfloat16)
    grad_fquery = jnp.einsum(
        "td,te->de", second_low, dquery_low, preferred_element_type=jnp.float32
    )
    dsecond = (
        dsecond_sum
        + jnp.einsum("te,de->td", dquery_low, merging_proj[0], preferred_element_type=jnp.float32)
        + dthird
    )
    dmid_rows, gain_second, shift_second = normalize_back(
        dsecond, unit_second, inverse_second, norm_gains[1]
    )
    dmid_low = dmid_rows.astype(jnp.bfloat16)
    grad_bias_out = jnp.sum(dmid_rows, 0)
    grad_out_ffn = jnp.einsum("tf,td->fd", inner, dmid_low, preferred_element_type=jnp.float32)
    dinner = gelu_back(
        inner_pre, jnp.einsum("td,fd->tf", dmid_low, ffn_out, preferred_element_type=jnp.float32)
    ).astype(jnp.bfloat16)
    grad_bias_in = jnp.sum(dinner.astype(jnp.float32), 0)
    grad_in_ffn = jnp.einsum("td,tf->df", first_low, dinner, preferred_element_type=jnp.float32)
    dfirst = (
        lax.psum(
            jnp.einsum("tf,df->td", dinner, ffn_in, preferred_element_type=jnp.float32).astype(
                jnp.bfloat16
            ),
            "ad",
        ).astype(jnp.float32)
        + dmid_rows
    )
    dlow, gain_first, shift_first = normalize_back(dfirst, unit_first, inverse_first, norm_gains[0])
    dlow_low = dlow.astype(jnp.bfloat16)
    grad_attended = jnp.einsum("tc,td->cd", context, dlow_low, preferred_element_type=jnp.float32)
    dcontext = jnp.einsum(
        "td,cd->tc", dlow_low, attn_out, preferred_element_type=jnp.float32
    ).astype(jnp.bfloat16)
    dpacked = lax.map(
        attend_back, (packed, log_totals, dcontext.reshape(sequences, positions, -1), keep)
    )
    grad_packed = jnp.einsum(
        "std,sjte->jde", seq_tokens, dpacked, preferred_element_type=jnp.float32
    )
    dtokens_part = jnp.einsum(
        "sjte,jde->std", dpacked, attn_qkv, preferred_element_type=jnp.float32
    ).reshape(row_count, model_width)
    grad_inputs = lax.psum(dtokens_part.astype(jnp.bfloat16), "ad").astype(jnp.float32) + dlow
    gains_grad = jnp.stack([gain_first, gain_second, gain_third])
    shifts_grad = jnp.stack([shift_first, shift_second, shift_third])
    summed = (
        lax.psum(grad_packed.astype(jnp.bfloat16), "tok").astype(jnp.float32),
        lax.psum(grad_attended.astype(jnp.bfloat16), "tok").astype(jnp.float32),
        lax.psum(grad_in_ffn.astype(jnp.bfloat16), "tok").astype(jnp.float32),
        lax.psum(grad_bias_in.astype(jnp.bfloat16), "tok").astype(jnp.float32),
        lax.psum(grad_out_ffn.astype(jnp.bfloat16), "tok").astype(jnp.float32),
        lax.psum(grad_bias_out.astype(jnp.bfloat16), "tok").astype(jnp.float32),
        lax.psum(gains_grad.astype(jnp.bfloat16), "tok").astype(jnp.float32),
        lax.psum(shifts_grad.astype(jnp.bfloat16), "tok").astype(jnp.float32),
        lax.psum(grad_fquery.astype(jnp.bfloat16), "tok").astype(jnp.float32),
        lax.psum(mass.astype(jnp.bfloat16), "tok").astype(jnp.float32),
        lax.psum(counted.astype(jnp.bfloat16), "tok").astype(jnp.float32),
        lax.psum(group_keys.astype(jnp.bfloat16), "tok").astype(jnp.float32),
        lax.psum(group_values.astype(jnp.bfloat16), "tok").astype(jnp.float32),
    )
    merging_grad = jnp.stack([summed[8], summed[11], summed[12]])
    usage = summed[9] / summed[10]
    return (
        output,
        grad_inputs,
        summed[0],
        summed[1],
        summed[2],
        summed[3],
        summed[4],
        summed[5],
        summed[6],
        summed[7],
        merging_grad,
        usage,
    )


def solution(mesh):
    placed = (
        P("tok", None),
        P("tok", None),
        P(None, None, "ad"),
        P("ad", None),
        P(None, "ad"),
        P("ad"),
        P("ad", None),
        P(),
        P(),
        P(),
        P(None, "ad"),
        P("ad", None, None),
        P(),
        P("tok", "ad"),
        P("tok"),
    )
    return jax.shard_map(
        on_device,
        mesh=mesh,
        in_specs=placed,
        out_specs=(
            P("tok", None),
            P("tok", None),
            P(None, None, "ad"),
            P("ad", None),
            P(None, "ad"),
            P("ad"),
            P("ad", None),
            P(),
            P(),
            P(),
            P(),
            P("ad"),
        ),
        check_vma=False,
    )
```

profile of v0, /device:TPU:0, one launch (start us, length us, event | category | flops | bytes accessed | tf_op | source)
XLA Modules:
  0.0 931.1 jit_solution(16041043972455983177)
XLA Ops:
  7.3 2.9 fusion.96
  11.3 15.3 %while.46 = (s32[]{:T(128)}, bf16[2,512,192]{1,2,0:T(8,128)(2,1)}, f32[2,3,512]{2,1,0:T(4,128)}, bf16[2,512,3,64]{1,3,2,0:T(8,128)(2,1)S(1)}, bf16[1024,3,64]{0,...) while((s32[]{:T(128)}, bf16[2,512,192]{1,2,0:T(8,128)(2,1)}, ...), condition=%wide.region_3.4_spmd.clone, body=%wide.region_0.3_spmd.clone.sunk | while | flops 421625344 | bytes 20503644 | solution.py:73
  15.3 3.0 fusion.229
  23.0 3.0 fusion.229
  28.8 2.7 convolution_convert_fusion.3
  33.1 44.1 %all-reduce.12.cloned.1.call-done = bf16[1024,768]{1,0:T(8,128)(2,1)} async-done(((bf16[1024,768]{1,0:T(8,128)(2,1)}), bf16[1024,768]{1,0:T(8,128)(2,1)}) %all-reduce.12.cloned.1.call-update) | async-done | bytes 1572880 | tf_op jit(solution)/shard_map/psum | solution.py:157
  77.2 2.0 fusion.81
  80.2 9.7 %multiply_convert_fusion.7 = (bf16[1024,768]{1,0:T(8,128)(2,1)S(1)}, f32[1024,768]{1,0:T(8,128)}, f32[1024,768]{1,0:T(8,128)}) fusion(f32[768]{0:T(1024)S(1)} %copy-done.81, bf16[768,768]{1,0:T(8,128)(2,1)S(1)} %copy-done, f32[768]{0:T(1024)S(1)} %copy-done.65, f32[768]{0:T(1024)S(1)} %get-tuple-element.331, f32[1024]{0:T(1024)S(1)} %add_rsqrt_fusion.2, ...), kind=kOutput, calls=%fused_computation.111 | convolution fusion | flops 1266155520 | bytes 12207104 | tf_op jit(solution)/shard_map/dot_general | solution.py:164
  91.0 3.1 fusion.167
  94.7 68.0 %all-reduce.14.cloned.1.call-done = f32[1024,768]{1,0:T(8,128)} async-done(((f32[1024,768]{1,0:T(8,128)}), f32[1024,768]{1,0:T(8,128)}) %all-reduce.14.cloned.1.call-update) | async-done | bytes 3145744 | tf_op jit(solution)/shard_map/psum | solution.py:167
  162.8 3.6 fusion.162
  168.2 3.2 multiply_convert_fusion.14
  171.5 1.9 fusion.52
  173.5 8.3 fusion.103
  181.7 5.3 convolution_convert_fusion
  187.1 3.7 fusion.165
  190.8 12.8 %fusion.63 = f32[1024,1,4]{2,1,0:T(1,128)S(1)} fusion(bf16[1024,4,768]{2,0,1:T(8,128)(2,1)S(1)} %convolution_convert_fusion, bf16[1024,768,1]{1,0,2:T(8,128)(2,1)S(1)} %bitcast.248), kind=kOutput, calls=%fused_computation.74 | convolution fusion | flops 6291456 | bytes 7880704 | tf_op jit(solution)/shard_map/td,tad->ta/dot_general | solution.py:195
  203.9 5.8 pmax.7
  211.2 35.4 %fusion.46 = bf16[1024,1,768]{2,1,0:T(2,128)(2,1)S(1)} fusion(f32[1024,4,1]{1,2,0:T(1,128)S(1)} %copy.43, f32[1024,4,768]{2,0,1:T(8,128)} %fusion.103), kind=kOutput, calls=%fused_computation.57 | convolution fusion | flops 37748736 | bytes 14172160 | tf_op jit(solution)/shard_map/ta,tad->td/dot_general | solution.py:200
  248.1 6.5 psum.164
  255.9 35.7 %all-reduce.16.cloned.1.call-done = bf16[1024,768]{1,0:T(8,128)(2,1)} async-done(((bf16[1024,768]{1,0:T(8,128)(2,1)}), bf16[1024,768]{1,0:T(8,128)(2,1)}) %all-reduce.16.cloned.1.call-update) | async-done | bytes 1572880 | tf_op jit(solution)/shard_map/psum | solution.py:203
  291.7 3.3 fusion.158
  296.4 1.9 fusion.71
  298.3 3.6 multiply_reduce_fusion.5
  301.9 1.7 copy-done.28
  303.7 51.6 %fusion.44 = f32[1024,1,4]{2,1,0:T(1,128)} fusion(f32[1024,4,768]{2,0,1:T(8,128)S(1)} %bitcast.241, f32[1024,768,1]{1,0,2:T(8,128)S(1)} %bitcast.247), kind=kOutput, calls=%fused_computation.55 | convolution fusion | flops 37748736 | bytes 15745024 | tf_op jit(solution)/shard_map/td,tad->ta/dot_general | solution.py:216
  355.3 1.8 copy.47
  358.4 1.7 copy.48
  360.1 17.2 %fusion.61 = bf16[1024,1,768]{2,1,0:T(2,128)(2,1)S(1)} fusion(f32[1024,4,1]{1,2,0:T(1,128)} %copy.48, bf16[1024,4,768]{2,0,1:T(8,128)(2,1)} %copy-done.86), kind=kOutput, calls=%fused_computation.72 | convolution fusion | flops 37748736 | bytes 7880704 | tf_op jit(solution)/shard_map/ta,tad->td/dot_general | solution.py:220
  379.8 9.6 %fusion.49 = f32[1024,4,768]{2,0,1:T(8,128)} fusion(f32[1024,768]{1,0:T(8,128)S(1)} %copy-done.27, f32[1024,4]{0,1:T(4,128)S(1)} %copy-done.62, bf16[3,768,768]{2,1,0:T(8,128)(2,1)} %param.31), kind=kOutput, calls=%fused_computation.60 | convolution fusion | flops 4838129664 | bytes 16924672 | tf_op jit(solution)/shard_map/tae,de->tad/dot_general | solution.py:222
  389.4 11.2 %convert_reduce_fusion = (f32[1024,768]{1,0:T(8,128)}, bf16[1024,4,768]{2,0,1:T(8,128)(2,1)S(1)}) fusion(f32[1024,4,768]{2,0,1:T(8,128)} %fusion.49, bf16[3,768,768]{2,1,0:T(8,128)(2,1)} %param.31, f32[1024,768]{1,0:T(8,128)S(1)} %copy-done.29, f32[1024,4]{0,1:T(4,128)S(1)} %copy-done.69), kind=kOutput, calls=%fused_computation.50 | convolution fusion | flops 4849926144 | bytes 26361856 | tf_op jit(solution)/shard_map/tae,de->tad/dot_general | solution.py:223
  400.6 1.9 fusion.168
  402.9 1.8 add_convert_fusion.3
  404.8 10.1 %bitcast_convert_fusion.4 = bf16[768,768]{1,0:T(8,128)(2,1)} fusion(bf16[1024,4,768]{2,0,1:T(8,128)(2,1)} %copy-done.23, f32[1024,768]{1,0:T(8,128)} %get-tuple-element.323, f32[1024,4]{0,1:T(4,128)} %get-tuple-element.299), kind=kOutput, calls=%fused_computation.138 | convolution fusion | flops 4838719488 | bytes 10633216 | tf_op jit(solution)/shard_map/tad,tae->de/dot_general | solution.py:225
  414.9 58.7 %all-reduce.24.cloned.1.call-done = (bf16[1024,768]{1,0:T(8,128)(2,1)}, bf16[1024,768]{1,0:T(8,128)(2,1)}) async-done(((bf16[1024,768]{1,0:T(8,128)(2,1)}, bf16[1024,768]{1,0:T(8,128)(2,1)}), (bf16[1024,768]{1,0:T(8,128)(2,1)}, bf16[1024,768]{1,0:T(8,128)(2,1)})) %all-reduce.24.cloned.1.call-update) | async-done | bytes 3145744 | tf_op jit(solution)/shard_map/psum | solution.py:240
  473.6 7.0 multiply_reduce_fusion.1
  482.9 2.1 copy-done.88
  485.0 2.9 fusion.166
  489.1 2.6 convolution_convert_fusion.1
  491.8 10.2 %bitcast_convert_fusion.3 = bf16[768,768]{1,0:T(8,128)(2,1)} fusion(bf16[1024,4,768]{2,0,1:T(8,128)(2,1)} %copy-done.23, f32[1024,768]{1,0:T(8,128)} %copy-done.28, f32[1024,4]{0,1:T(4,128)} %get-tuple-element.300), kind=kOutput, calls=%fused_computation.137 | convolution fusion | flops 4838719488 | bytes 10633216 | tf_op jit(solution)/shard_map/tad,tae->de/dot_general | solution.py:226
  501.9 32.9 %all-reduce.18.cloned.1.call-done = bf16[1024,768]{1,0:T(8,128)(2,1)} async-done(((bf16[1024,768]{1,0:T(8,128)(2,1)}), bf16[1024,768]{1,0:T(8,128)(2,1)}) %all-reduce.18.cloned.1.call-update) | async-done | bytes 1572880 | tf_op jit(solution)/shard_map/psum | solution.py:263
  534.8 5.6 multiply_reduce_fusion.2
  544.8 35.0 %while.47 = (s32[]{:T(128)}, f32[1024,3,64]{0,2,1:T(8,128)S(1)}, f32[1024,3,64]{0,2,1:T(8,128)}, bf16[2,512,3,64]{1,3,2,0:T(8,128)(2,1)}, bf16[2,512,3,64]{1,3,2...) while((s32[]{:T(128)}, f32[1024,3,64]{0,2,1:T(8,128)S(1)}, ...), condition=%wide.region_30.31_spmd.clone, body=%wide.region_28.30_spmd.clone.sunk | while | flops 1031306752 | bytes 106219792 | solution.py:116
  547.3 3.3 multiply_reduce_fusion.12
  550.6 2.9 multiply_convert_fusion.16
  553.5 2.8 fusion.240
  556.3 3.0 fusion.242
  559.3 2.4 fusion.241
  564.2 3.3 multiply_reduce_fusion.12
  567.5 2.9 multiply_convert_fusion.16
  570.4 2.8 fusion.240
  573.2 3.0 fusion.242
  576.2 3.7 fusion.241
  582.7 3.7 bitcast_convert_fusion
  586.8 5.0 fusion.95
  591.9 2.5 convolution_convert_fusion.5
  594.9 3.0 convolution_convert_fusion.6
  599.1 2.0 fusion.99
  601.1 67.2 %all-reduce.22.cloned.1.call-done = (bf16[1024,768]{1,0:T(8,128)(2,1)}, bf16[768,768]{1,0:T(8,128)(2,1)}, bf16[768,768]{1,0:T(8,128)(2,1)}) async-done(((bf16[1024,768]{1,0:T(8,128)(2,1)}, bf16[768,768]{1,0:T(8,128)(2,1)}, bf16[768,768]{1,0:T(8,128)(2,1)}), (bf16[1024,768]{1,0:T(8,128)(2,1)}, bf16[768,768]{1,0:T(8,128)(2,1)}, bf16[768,768]{1,0:T(8,128)(2,1)})) %all-reduce.22.cloned.1.call-update) | async-done | bytes 3932176 | tf_op jit(solution)/shard_map/psum | solution.py:286
  670.4 39.3 %all-reduce = (bf16[768]{0:T(1024)(128)(2,1)S(1)}, bf16[768]{0:T(1024)(128)(2,1)S(1)}, bf16[3,768]{1,0:T(4,128)(2,1)S(1)}, bf16[3,768]{1,0:T(4,128)(2,1)S(1)}, bf16[4]{0:T(256)(128)(2,1)S(1)}, /*index=5*/bf16[]{:T(256)}) all-reduce(bf16[768]{0:T(1024)(128)(2,1)S(1)} %copy-done.76, ...), channel_id=1, replica_groups=mesh['tok'=8,'ad'=4] {'tok'}, use_global_device_ids=true, to_apply=%region_36.37 | all-reduce | flops 6149 | bytes 24596 | tf_op jit(solution)/shard_map/psum | solution.py:293
  713.3 4.6 convert_add_fusion
  717.8 195.6 %all-reduce.20.cloned.1.call-done = (bf16[3,768,192]{1,2,0:T(8,128)(2,1)}, bf16[192,768]{1,0:T(8,128)(2,1)}, bf16[768,768]{1,0:T(8,128)(2,1)}, bf16[768,768]{1,0...) async-done(((bf16[3,768,192]{1,2,0:T(8,128)(2,1)}, bf16[192,768]{1,0:T(8,128)(2,1)}, ...) | async-done | bytes 7077904 | tf_op jit(solution)/shard_map/psum | solution.py:290
  913.4 3.0 convert_element_type.263
  920.3 3.5 maximum_convert_fusion
  (293 shorter events, 54.6 us)
Async XLA Ops:
  7.2 72.9 %copy-start = (bf16[768,768]{1,0:T(8,128)(2,1)S(1)}, bf16[768,768]{1,0:T(8,128)(2,1)}, u32[]{:S(2)}) copy-start(bf16[768,768]{1,0:T(8,128)(2,1)} %param.23) | copy-start | bytes 3538948
  7.2 70.0 %all-reduce.12.cloned.1.call-start = ((), (), s32[]{:S(2)}) async-start(), calls=%async_computation | async-start | bytes 3145728 | tf_op jit(solution)/shard_map/psum | solution.py:157
  26.6 52.6 %copy-start.3 = (bf16[1024,3,64]{0,2,1:T(8,128)(2,1)}, bf16[1024,3,64]{0,2,1:T(8,128)(2,1)S(1)}, u32[]{:S(2)}) copy-start(bf16[1024,3,64]{0,2,1:T(8,128)(2,1)S(1)} %get-tuple-element.533) | copy-start | bytes 1179652
  26.7 52.6 %copy-start.14 = (bf16[2,512,3,64]{1,3,2,0:T(8,128)(2,1)}, bf16[2,512,3,64]{1,3,2,0:T(8,128)(2,1)S(1)}, u32[]{:S(2)}) copy-start(bf16[2,512,3,64]{1,3,2,0:T(8,128)(2,1)S(1)} %get-tuple-element.535) | copy-start | bytes 1179652
  26.7 50.6 %copy-start.9 = (bf16[1024,768]{1,0:T(8,128)(2,1)S(1)}, bf16[1024,768]{1,0:T(8,128)(2,1)}, u32[]{:S(2)}) copy-start(bf16[1024,768]{1,0:T(8,128)(2,1)} %param.19) | copy-start | bytes 4718596
  31.5 131.2 %all-reduce.14.cloned.1.call-start = ((), (), s32[]{:S(2)}) async-start(), calls=%async_computation.1 | async-start | bytes 6291456 | tf_op jit(solution)/shard_map/psum | solution.py:167
  33.1 129.7 %copy-start.54 = (f32[768]{0:T(1024)}, f32[768]{0:T(1024)S(1)}, u32[]{:S(2)}) copy-start(f32[768]{0:T(1024)S(1)} %get-tuple-element.331) | copy-start | bytes 9220
  33.1 133.9 %copy-start.59 = (f32[768]{0:T(1024)}, f32[768]{0:T(1024)S(1)}, u32[]{:S(2)}) copy-start(f32[768]{0:T(1024)S(1)} %get-tuple-element.330) | copy-start | bytes 9220
  33.1 133.9 %copy-start.64 = (f32[768]{0:T(1024)}, f32[768]{0:T(1024)S(1)}, u32[]{:S(2)}) copy-start(f32[768]{0:T(1024)S(1)} %get-tuple-element.246) | copy-start | bytes 9220
  77.2 2.9 copy-start.65
  77.2 2.9 copy-start.81
  79.3 83.5 %copy-start.47 = (f32[1024]{0:T(1024)}, f32[1024]{0:T(1024)S(1)}, u32[]{:S(2)}) copy-start(f32[1024]{0:T(1024)S(1)} %broadcast_multiply_fusion.8) | copy-start | bytes 12292
  80.1 82.7 %copy-start.51 = (f32[1024]{0:T(1024)}, f32[1024]{0:T(1024)S(1)}, u32[]{:S(2)}) copy-start(f32[1024]{0:T(1024)S(1)} %add_rsqrt_fusion.2) | copy-start | bytes 12292
  80.1 10.9 %copy-start.79 = (bf16[768,768]{1,0:T(8,128)(2,1)S(1)}, bf16[768,768]{1,0:T(8,128)(2,1)}, u32[]{:S(2)}) copy-start(bf16[768,768]{1,0:T(8,128)(2,1)} %param.25) | copy-start | bytes 3538948
  94.1 68.7 %copy-start.66 = (f32[768]{0:T(1024)S(1)}, f32[768]{0:T(1024)}, u32[]{:S(2)}) copy-start(f32[768]{0:T(1024)} %get-tuple-element.245) | copy-start | bytes 9220
  94.1 68.7 %copy-start.75 = (f32[768]{0:T(1024)S(1)}, f32[768]{0:T(1024)}, u32[]{:S(2)}) copy-start(f32[768]{0:T(1024)} %param.26) | copy-start | bytes 9220
  94.1 197.6 %all-reduce.16.cloned.1.call-start = ((), (), s32[]{:S(2)}) async-start(), calls=%async_computation.2 | async-start | bytes 3145728 | tf_op jit(solution)/shard_map/psum | solution.py:203
  168.2 18.9 %copy-start.16 = (f32[1024,768]{1,0:T(8,128)}, f32[1024,768]{1,0:T(8,128)S(1)}, u32[]{:S(2)}) copy-start(f32[1024,768]{1,0:T(8,128)S(1)} %multiply_add_fusion) | copy-start | bytes 9437188
  168.2 3.2 copy-start.31
  173.5 8.3 copy-start.23
  187.1 3.7 copy-start.86
  248.0 225.5 %all-reduce.24.cloned.1.call-start = ((), (), s32[]{:S(2)}) async-start(), calls=%async_computation.6 | async-start | bytes 6291456 | tf_op jit(solution)/shard_map/psum | solution.py:240
  291.7 11.9 %slice-start = ((s8[12582912]{0:T(1024)(128)(4,1)}), s8[4194304]{0:T(1024)(128)(4,1)S(1)}, s32[]{:S(2)}) async-start(s8[12582912]{0:T(1024)(128)(4,1)} %bitcast.240), calls=%async_computation.7 | async-start | bytes 8388608
  295.0 8.6 slice-start.1
  295.5 2.8 copy-start.24
  295.5 2.8 copy-start.61
  298.3 5.3 slice-start.2
  379.8 9.6 %copy-start.29 = (f32[1024,768]{1,0:T(8,128)S(1)}, f32[1024,768]{1,0:T(8,128)}, u32[]{:S(2)}) copy-start(f32[1024,768]{1,0:T(8,128)} %copy-done.28) | copy-start | bytes 9437188
  379.8 9.6 %copy-start.69 = (f32[1024,4]{0,1:T(4,128)S(1)}, f32[1024,4]{0,1:T(4,128)}, u32[]{:S(2)}) copy-start(f32[1024,4]{0,1:T(4,128)} %get-tuple-element.300) | copy-start | bytes 49156
  389.4 11.2 %copy-start.32 = (bf16[4,48,768]{2,1,0:T(8,128)(2,1)S(1)}, bf16[4,48,768]{2,1,0:T(8,128)(2,1)}, u32[]{:S(2)}) copy-start(bf16[4,48,768]{2,1,0:T(8,128)(2,1)} %param.30) | copy-start | bytes 884740
  404.7 68.8 %copy-start.50 = (f32[1024]{0:T(1024)S(1)}, f32[1024]{0:T(1024)}, u32[]{:S(2)}) copy-start(f32[1024]{0:T(1024)} %copy-done.49) | copy-start | bytes 12292
  404.7 68.8 %copy-start.58 = (f32[1024]{0:T(1024)S(1)}, f32[1024]{0:T(1024)}, u32[]{:S(2)}) copy-start(f32[1024]{0:T(1024)} %copy-done.57) | copy-start | bytes 12292
  404.8 68.8 %copy-start.60 = (f32[768]{0:T(1024)S(1)}, f32[768]{0:T(1024)}, u32[]{:S(2)}) copy-start(f32[768]{0:T(1024)} %copy-done.59) | copy-start | bytes 9220
  404.8 130.0 %all-reduce.18.cloned.1.call-start = ((), (), s32[]{:S(2)}) async-start(), calls=%async_computation.3 | async-start | bytes 3145728 | tf_op jit(solution)/shard_map/psum | solution.py:263
  473.6 7.1 copy-start.6
  480.7 4.3 copy-start.88
  482.0 5.9 copy-start.17
  491.7 43.1 %copy-start.48 = (f32[1024]{0:T(1024)S(1)}, f32[1024]{0:T(1024)}, u32[]{:S(2)}) copy-start(f32[1024]{0:T(1024)} %copy-done.47) | copy-start | bytes 12292
  491.7 43.1 %copy-start.52 = (f32[1024]{0:T(1024)S(1)}, f32[1024]{0:T(1024)}, u32[]{:S(2)}) copy-start(f32[1024]{0:T(1024)} %copy-done.51) | copy-start | bytes 12292
  491.7 43.1 %copy-start.55 = (f32[768]{0:T(1024)S(1)}, f32[768]{0:T(1024)}, u32[]{:S(2)}) copy-start(f32[768]{0:T(1024)} %copy-done.54) | copy-start | bytes 9220
  491.7 176.6 %all-reduce.22.cloned.1.call-start = ((), (), s32[]{:S(2)}) async-start(), calls=%async_computation.5 | async-start | bytes 7864320 | tf_op jit(solution)/shard_map/psum | solution.py:286
  534.8 5.6 copy-start.12
  534.8 5.6 copy-start.18
  534.8 5.6 copy-start.22
  540.4 3.2 copy-start.37
  545.8 4.8 copy-start.1
  550.6 5.7 copy-start.42
  553.5 5.8 copy-start.2
  562.7 4.8 copy-start.1
  567.5 5.7 copy-start.42
  570.4 5.8 copy-start.2
  576.1 3.7 copy-start.43
  586.5 326.9 %all-reduce.20.cloned.1.call-start = ((), (), s32[]{:S(2)}) async-start(), calls=%async_computation.4 | async-start | bytes 14155776 | tf_op jit(solution)/shard_map/psum | solution.py:290
  586.8 5.0 copy-start.19
  586.8 5.0 copy-start.85
  591.9 3.1 copy-start.90
  594.9 3.0 copy-start.8
  594.9 3.0 copy-start.26
  913.4 3.0 copy-start.33
  913.4 4.6 copy-start.38
  916.4 3.0 copy-start.44
  916.4 3.8 copy-start.34
  916.4 3.8 copy-start.35
  916.5 3.8 copy-start.36
  (41 other events, 75.2 us)
Sparse Core Ops, SparseCore 0:
  31.7 45.5 all-reduce.11
  94.2 68.4 all-reduce.13
  248.2 43.4 all-reduce.15
  404.9 68.6 all-reduce.23
  491.8 42.9 all-reduce.17
  586.6 81.6 all-reduce.21
  674.8 238.6 all-reduce.19
where the time goes:
time: 939 us; the launch traced here: 931 us
  waiting for transfers between devices  502 us (53%)
  matrix products  268 us (29%)
  other arithmetic  61.2 us (7%)
  blocking collectives  51.6 us (5%)
  local copies, waits for them, and re-layouts  30.3 us (3%)
  between operations  17 us (2%)
    psum x1, waiting for transfers between devices, on_device(): lax.psum(grad_packed.astype(jnp.bfloat16), 'tok').astype(jnp.float32)  196 us
    psum x1, waiting for transfers between devices, on_device(): lax.psum(jnp.dot(inner, ffn_out, preferred_element_type=jnp.float32), 'ad')  68 us
    psum x1, waiting for transfers between devices, on_device(): lax.psum(dtokens_part.astype(jnp.bfloat16), 'ad').astype(jnp.float32) + dlow  67.2 us
    psum x1, waiting for transfers between devices, on_device(): lax.psum(dsecond_part.astype(jnp.bfloat16), 'ad').astype(jnp.float32)  58.7 us
    dot_general x1, matrix products, on_device(): dprobs = jnp.einsum('td,tad->ta', dthird, fvalues, precision=HIGHEST)  51.6 us
    psum x1, waiting for transfers between devices, on_device(): lax.psum(jnp.dot(context, attn_out, preferred_element_type=jnp.float32).a...  44.1 us
    psum x1, blocking collectives, on_device(): lax.psum(grad_bias_in.astype(jnp.bfloat16), 'tok').astype(jnp.float32)  39.3 us
    psum x1, waiting for transfers between devices, on_device(): lax.psum(local_mix.astype(jnp.bfloat16), 'ad').astype(jnp.float32)  35.7 us
  transfers between devices with their start and end apart: 7, of which 7 were waited for; matrix products, arithmetic and copies ran while one was open for 5% of the time, Pallas kernels for 0%

commit v1 on v0

v1 whole, which is shorter than its diff:
```python
import jax
import jax.numpy as jnp
from jax import lax
from jax.sharding import PartitionSpec as P

HEAD = 64
EPSILON = 1e-06
NEGATIVE = -1e30
BLOCK_LIMIT = 512
F32 = jnp.float32
BF16 = jnp.bfloat16


def normalize(values, gain, shift):
    centred = values - jnp.mean(values, -1, keepdims=True)
    inverse = lax.rsqrt(jnp.mean(centred * centred, -1, keepdims=True) + EPSILON)
    unit_rows = centred * inverse
    return (unit_rows * gain + shift, unit_rows, inverse)


def normalize_back(gradient, unit_rows, inverse, gain):
    scaled = gradient * gain
    centred = (
        scaled
        - jnp.mean(scaled, -1, keepdims=True)
        - unit_rows * jnp.mean(scaled * unit_rows, -1, keepdims=True)
    )
    return (centred * inverse, jnp.sum(gradient * unit_rows, 0), jnp.sum(gradient, 0))


def gelu_both(values):
    cdf = 0.5 * (1.0 + lax.erf(values * 0.7071067811865476))
    density = jnp.exp(-0.5 * values * values) * 0.3989422804014327
    return values * cdf, cdf + values * density


def dot(left, right, dims=((1,), (0,))):
    return lax.dot_general(left, right, (dims, ((), ())), preferred_element_type=F32)


def dot_nt(left, right):
    return dot(left, right, ((1,), (1,)))


def dot_tn(left, right):
    return dot(left, right, ((0,), (0,)))


def split_dot(left, right):
    high = left.astype(BF16)
    rest = (left - high.astype(F32)).astype(BF16)
    return dot(high, right) + dot(rest, right)


def swap(array, axis, size, step):
    return lax.ppermute(array, axis, [(i, i ^ step) for i in range(size)])


def gather_xor(block):
    across = swap(block, "ad", 4, 2)
    beside = swap(block, "ad", 4, 1)
    return [block, beside, across, swap(across, "ad", 4, 1)]


def scatter_xor(parts):
    dtype = parts[0].dtype
    beside = swap(jnp.stack([parts[1], parts[3]]), "ad", 4, 1)
    own = parts[0].astype(F32) + beside[0].astype(F32)
    across = (parts[2].astype(F32) + beside[1].astype(F32)).astype(dtype)
    return own + swap(across, "ad", 4, 2).astype(F32)


def exchange_xor(parts):
    across = swap(jnp.stack([parts[2], parts[3]]), "ad", 4, 2)
    beside = swap(jnp.stack([parts[1], across[1]]), "ad", 4, 1)
    return [parts[0], beside[0], across[0], beside[1]]


def to_xor(blocks, me):
    return [lax.dynamic_index_in_dim(blocks, me ^ k, 0, keepdims=False) for k in range(4)]


def attend(packed, keep):
    positions = packed.shape[1]
    heads = packed.shape[2] // HEAD
    block_rows = min(BLOCK_LIMIT, positions)
    key_rows = packed[1].reshape(positions, heads, HEAD)
    value_rows = packed[2].reshape(positions, heads, HEAD)
    queries = packed[0].reshape(positions // block_rows, block_rows, heads, HEAD)
    scaling = HEAD ** (-0.5)

    def one_block(query_rows):
        logits = (
            jnp.einsum("qhd,khd->hqk", query_rows, key_rows, preferred_element_type=F32) * scaling
        )
        logits = jnp.where(keep[None, None, :], logits, NEGATIVE)
        highest = jnp.max(logits, -1, keepdims=True)
        expon = jnp.exp(logits - highest)
        totals = jnp.sum(expon, -1, keepdims=True)
        weights = (expon / totals).astype(BF16)
        context = jnp.einsum("hqk,khd->qhd", weights, value_rows, preferred_element_type=F32)
        return (
            context.astype(BF16).reshape(block_rows, -1),
            (highest + jnp.log(totals))[:, :, 0],
        )

    context, log_totals = lax.map(one_block, queries)
    return (context.reshape(positions, -1), log_totals)


def attend_back(packed, log_totals, grad_context, keep):
    positions = packed.shape[1]
    heads = packed.shape[2] // HEAD
    block_rows = min(BLOCK_LIMIT, positions)
    key_rows = packed[1].reshape(positions, heads, HEAD)
    value_rows = packed[2].reshape(positions, heads, HEAD)
    queries = packed[0].reshape(positions // block_rows, block_rows, heads, HEAD)
    scaling = HEAD ** (-0.5)
    gradients = grad_context.reshape(queries.shape)

    def one_block(carried, pieces):
        query_rows, log_block, grad_block = pieces
        logits = (
            jnp.einsum("qhd,khd->hqk", query_rows, key_rows, preferred_element_type=F32) * scaling
        )
        logits = jnp.where(keep[None, None, :], logits, NEGATIVE)
        probs = jnp.exp(logits - log_block[:, :, None])
        grad_probs = jnp.einsum("qhd,khd->hqk", grad_block, value_rows, preferred_element_type=F32)
        inner_sum = jnp.sum(probs * grad_probs, -1, keepdims=True)
        grad_logits = (probs * (grad_probs - inner_sum)).astype(BF16)
        grad_query = (
            jnp.einsum("hqk,khd->qhd", grad_logits, key_rows, preferred_element_type=F32) * scaling
        )
        grad_keys = (
            carried[0]
            + jnp.einsum("hqk,qhd->khd", grad_logits, query_rows, preferred_element_type=F32)
            * scaling
        )
        grad_values = carried[1] + jnp.einsum(
            "hqk,qhd->khd", probs.astype(BF16), grad_block, preferred_element_type=F32
        )
        return ((grad_keys, grad_values), grad_query)

    zero_rows = jnp.zeros(key_rows.shape, F32)
    (grad_keys, grad_values), grad_query = lax.scan(
        one_block, (zero_rows, zero_rows), (queries, log_totals, gradients)
    )
    return jnp.stack(
        [
            grad_query.reshape(positions, -1),
            grad_keys.reshape(positions, -1),
            grad_values.reshape(positions, -1),
        ]
    ).astype(BF16)


def merge(second, second_low, down, up, merging, usable, valid, expand, gains, shifts, cot):
    width = second.shape[1]
    scaling = width ** (-0.5)
    collect = expand.T
    bottle = dot(second_low, down)
    squeezed, slope = gelu_both(bottle)
    squeezed = squeezed.astype(BF16).astype(F32)
    fquery = dot(second_low, merging[0]).astype(BF16)
    asked = dot_nt(fquery, merging[1])
    asked_up = dot_nt(asked.astype(BF16), up)
    scores = scaling * (
        jnp.sum(asked * second, -1, keepdims=True) + split_dot(squeezed * asked_up, collect)
    )
    scores = jnp.where(usable, scores, NEGATIVE)
    highest = jnp.max(scores, -1, keepdims=True)
    weights = jnp.where(usable, jnp.exp(scores - highest), 0.0)
    probs = weights / jnp.sum(weights, -1, keepdims=True)
    total = jnp.sum(probs, -1, keepdims=True)
    probs_wide = split_dot(probs, expand)
    mixed = total * second + dot((probs_wide * squeezed).astype(BF16), up)
    mixed_low = mixed.astype(BF16)
    blended = dot(mixed_low, merging[2])
    final, unit, inverse = normalize(second + blended, gains[2], shifts[2])
    mass = jnp.sum(probs * valid, 0)
    dthird, gain_third, shift_third = normalize_back(cot, unit, inverse, gains[2])
    dthird_low = dthird.astype(BF16)
    pulled = dot_nt(dthird_low, merging[2])
    pulled_up = dot_nt(pulled.astype(BF16), up)
    dprobs = jnp.sum(pulled * second, -1, keepdims=True) + split_dot(squeezed * pulled_up, collect)
    dscores = probs * (dprobs - jnp.sum(probs * dprobs, -1, keepdims=True)) * scaling
    dscores_total = jnp.sum(dscores, -1, keepdims=True)
    dscores_wide = split_dot(dscores, expand)
    weighed = dscores_total * second + dot((dscores_wide * squeezed).astype(BF16), up)
    weighed_low = weighed.astype(BF16)
    dquery = dot(weighed_low, merging[1]).astype(BF16)
    dbottle = ((dscores_wide * asked_up + probs_wide * pulled_up) * slope).astype(BF16)
    dsecond = (
        dthird
        + dscores_total * asked
        + total * pulled
        + dot_nt(dbottle, down)
        + dot_nt(dquery, merging[0])
    )
    grads = jnp.stack(
        [
            dot_tn(second_low, dquery),
            dot_tn(weighed_low, fquery),
            dot_tn(mixed_low, dthird_low),
        ]
    )
    return final.astype(BF16), dsecond, grads, gain_third, shift_third, mass


def on_device(
    tokens,
    cotangent,
    attn_qkv,
    attn_out,
    ffn_in,
    ffn_bias_in,
    ffn_out,
    ffn_bias_out,
    norm_gains,
    norm_shifts,
    adapter_down,
    adapter_up,
    merging_proj,
    adapter_mask,
    lengths,
):
    me = lax.axis_index("ad")
    row_count, width = tokens.shape
    block = row_count // 4
    out_blocks = gather_xor(attn_out)
    down_blocks = gather_xor(adapter_down)
    up_blocks = gather_xor(adapter_up.reshape(-1, width))
    mask_blocks = gather_xor(adapter_mask.astype(F32))
    out_whole = jnp.concatenate(out_blocks, 0)
    down = jnp.concatenate(down_blocks, 1)
    up = jnp.concatenate(up_blocks, 0)
    mask_row = jnp.concatenate(mask_blocks, 1)
    adapters = mask_row.shape[1]
    rank = up.shape[0] // adapters
    expand = (
        jnp.arange(adapters)[:, None] == jnp.arange(adapters * rank)[None, :] // rank
    ).astype(BF16)

    tokens = jnp.concatenate(to_xor(tokens.reshape(4, block, width), me), 0)
    positions = jnp.concatenate([(me ^ k) * block + jnp.arange(block) for k in range(4)])
    keep = positions < lengths[0]
    packed = jnp.einsum("td,jde->jte", tokens, attn_qkv, preferred_element_type=F32).astype(BF16)
    context, log_totals = attend(packed, keep)
    columns = [context.reshape(4, block, -1)]
    for k, other in enumerate(gather_xor(context)[1:], 1):
        other = other.reshape(4, block, -1)
        columns.append(jnp.stack([other[j ^ k] for j in range(4)]))
    context_whole = jnp.concatenate(columns, 2).reshape(row_count, -1)
    attended = dot(context_whole, out_whole)
    first, unit_first, inverse_first = normalize(
        tokens.astype(F32) + attended, norm_gains[0], norm_shifts[0]
    )
    first_low = first.astype(BF16)
    inner_pre = dot(first_low, ffn_in) + ffn_bias_in
    inner, inner_slope = gelu_both(inner_pre)
    inner = inner.astype(BF16)
    inner_slope = inner_slope.astype(BF16)
    fed = dot(inner, ffn_out).astype(BF16).reshape(4, block, width)
    fed_rows = scatter_xor([fed[k] for k in range(4)]) + ffn_bias_out
    second, unit_second, inverse_second = normalize(
        first[:block] + fed_rows, norm_gains[1], norm_shifts[1]
    )
    second_low = second.astype(BF16)
    cot = lax.dynamic_slice_in_dim(cotangent, me * block, block).astype(F32)
    valid = keep[:block, None].astype(F32)
    output_block, dsecond, merging_grads, gain_third, shift_third, mass = merge(
        second,
        second_low,
        down,
        up,
        merging_proj,
        mask_row > 0.5,
        valid,
        expand,
        norm_gains,
        norm_shifts,
        cot,
    )
    output = lax.all_gather(output_block, "ad", axis=0, tiled=True)
    group_merging = lax.psum_scatter(
        merging_grads.astype(BF16).reshape(-1, width), "ad", scatter_dimension=0, tiled=True
    )
    group_merging = lax.psum(group_merging, "tok")
    dmid, gain_second, shift_second = normalize_back(
        dsecond, unit_second, inverse_second, norm_gains[1]
    )
    grad_bias_out = jnp.sum(dmid, 0)
    dmid_low = jnp.concatenate(gather_xor(dmid.astype(BF16)), 0)
    grad_ffn_out = dot_tn(inner, dmid_low)
    dinner = (dot_nt(dmid_low, ffn_out) * inner_slope.astype(F32)).astype(BF16)
    grad_bias_in = jnp.sum(dinner.astype(F32), 0)
    grad_ffn_in = dot_tn(first_low, dinner)
    dfirst = dot_nt(dinner, ffn_in).astype(BF16).reshape(4, block, width)
    dfirst = scatter_xor([dfirst[k] for k in range(4)]) + dmid
    dlow, gain_first, shift_first = normalize_back(
        dfirst, unit_first[:block], inverse_first[:block], norm_gains[0]
    )
    dlow_low = dlow.astype(BF16)
    own_context = context_whole[:block]
    grad_attn_out = dot_tn(own_context, dlow_low).astype(BF16).reshape(4, -1, width)
    grad_attn_out = scatter_xor([grad_attn_out[k] for k in range(4)]).astype(BF16)
    dcontext = dot_nt(dlow_low, out_whole).astype(BF16)
    lanes = dcontext.shape[1] // 4
    dcontext = jnp.concatenate(
        exchange_xor([dcontext[:, k * lanes : (k + 1) * lanes] for k in range(4)]), 0
    )
    dpacked = attend_back(packed, log_totals, dcontext, keep)
    grad_packed = jnp.einsum("td,jte->jde", tokens, dpacked, preferred_element_type=F32)
    dtokens = (
        jnp.einsum("jte,jde->td", dpacked, attn_qkv, preferred_element_type=F32)
        .astype(BF16)
        .reshape(4, block, width)
    )
    dtokens = scatter_xor([dtokens[k] for k in range(4)]) + dlow
    grad_tokens = lax.all_gather(dtokens.astype(BF16), "ad", axis=0, tiled=True).astype(F32)

    grad_merging = lax.all_gather(group_merging, "ad", axis=0, tiled=True)
    grad_merging = grad_merging.reshape(3, width, width).astype(F32)
    low = [
        lax.psum(a.astype(BF16), "tok").astype(F32)
        for a in (grad_packed, grad_attn_out, grad_ffn_in, grad_ffn_out)
    ]
    small = jnp.stack(
        [
            gain_first,
            gain_second,
            gain_third,
            shift_first,
            shift_second,
            shift_third,
            grad_bias_out,
        ]
    )
    counted = jnp.sum(lengths.astype(F32))
    held = adapters // 4
    mass = jnp.concatenate(to_xor(mass.reshape(4, held), me))
    small, mass = lax.psum((small, mass), ("tok", "ad"))
    grad_bias_in, counted = lax.psum((grad_bias_in, counted), "tok")
    usage = lax.dynamic_slice_in_dim(mass, me * held, held) / counted
    return (
        output,
        grad_tokens,
        low[0],
        low[1],
        low[2],
        grad_bias_in,
        low[3],
        small[6],
        small[0:3],
        small[3:6],
        grad_merging,
        usage,
    )


def solution(mesh):
    placed = (
        P("tok", None),
        P("tok", None),
        P(None, None, "ad"),
        P("ad", None),
        P(None, "ad"),
        P("ad"),
        P("ad", None),
        P(),
        P(),
        P(),
        P(None, "ad"),
        P("ad", None, None),
        P(),
        P("tok", "ad"),
        P("tok"),
    )
    return jax.shard_map(
        on_device,
        mesh=mesh,
        in_specs=placed,
        out_specs=(
            P("tok", None),
            P("tok", None),
            P(None, None, "ad"),
            P("ad", None),
            P(None, "ad"),
            P("ad"),
            P("ad", None),
            P(),
            P(),
            P(),
            P(),
            P("ad"),
        ),
        check_vma=False,
    )
```

time: 939 us -> 473 us (0.50)
  waiting for transfers between devices: 502 us -> 219 us
  matrix products: 268 us -> 72.4 us
  starting transfers between devices: 0.75 us -> 19.8 us
  other arithmetic: 61.2 us -> 49.3 us
    psum x7 -> x1, waiting for transfers between devices: 502 us -> 146 us  [on_device(): lax.psum(a.astype(BF16), 'tok').astype(F32)]
    dot_general x38 -> x42, matrix products: 249 us -> 58.1 us  [the longest x32 39.3 us: dot(): lax.dot_general(left, right, (dims, ((), ())), preferred_element_type=F32)]
    ppermute x0 -> x28, waiting for transfers between devices: none -> 67.2 us  [swap(): return lax.ppermute(array, axis, [(i, i ^ step) for i in range(size)])]
    ppermute x0 -> x28, starting transfers between devices: none -> 19.6 us  [swap(): return lax.ppermute(array, axis, [(i, i ^ step) for i in range(size)])]
    psum x2, blocking collectives: 45.8 us -> 58.2 us  [the longest x1 37.4 us: on_device(): small, mass = lax.psum((small, mass), ('tok', 'ad'))]
    convert_element_type x12 -> x17, other arithmetic: 16.5 us -> 26.5 us  [the longest x1 5.71 us: on_device(): grad_merging = grad_merging.reshape(3, width, width).astype(F32)]
  transfers between devices with their start and end apart: 7 -> 33, of which waited for: 7 -> 14; matrix products, arithmetic and copies ran while one was open for 5% -> 18% of each run, Pallas kernels for 0% -> 0%
where the time goes in v1:
time: 473 us; the launch traced here: 466 us
  waiting for transfers between devices  219 us (46%)
  matrix products  72.4 us (15%)
  blocking collectives  58.2 us (12%)
  other arithmetic  49.3 us (10%)
  local copies, waits for them, and re-layouts  29.6 us (6%)
  starting transfers between devices  19.8 us (4%)
  between operations  16.5 us (3%)
    psum x1, waiting for transfers between devices, on_device(): lax.psum(a.astype(BF16), 'tok').astype(F32)  146 us
    ppermute x28, waiting for transfers between devices, swap(): return lax.ppermute(array, axis, [(i, i ^ step) for i in range(size)])  67.2 us
    dot_general x32, matrix products, dot(): lax.dot_general(left, right, (dims, ((), ())), preferred_element_type=F32)  39.3 us
    psum x1, blocking collectives, on_device(): small, mass = lax.psum((small, mass), ('tok', 'ad'))  37.4 us
    psum x1, blocking collectives, on_device(): grad_bias_in, counted = lax.psum((grad_bias_in, counted), 'tok')  20.8 us
    ppermute x28, starting transfers between devices, swap(): return lax.ppermute(array, axis, [(i, i ^ step) for i in range(size)])  19.6 us
    unnamed x226, local copies, waits for them, and re-layouts  14.7 us
  transfers between devices with their start and end apart: 33, of which 14 were waited for; matrix products, arithmetic and copies ran while one was open for 18% of the time, Pallas kernels for 0%

profile of v1, /device:TPU:0, one launch (start us, length us, event | category | flops | bytes accessed | tf_op | source)
XLA Modules:
  0.0 465.6 jit_solution(1384321630086953800)
XLA Ops:
  7.3 1.6 dynamic-slice_bitcast_fusion.4
  11.5 11.2 %while.27 = (s32[]{:T(128)}, bf16[2,512,192]{1,2,0:T(8,128)(2,1)}, f32[2,3,512]{2,1,0:T(4,128)}, pred[1024]{0:T(1024)(128)(4,1)S(1)}, bf16[2,512,3,64]{1,3,2,0:T...) while((s32[]{:T(128)}, bf16[2,512,192]{1,2,0:T(8,128)(2,1)}, ...), condition=%wide.region_3.4_spmd, body=%wide.region_0.3_spmd.sunk | while | flops 421624320 | bytes 23749840 | solution.py:107
  12.6 1.6 fusion.243
  14.3 2.0 fusion.244
  18.2 1.6 fusion.243
  19.8 2.0 fusion.244
  24.2 2.6 collective-permute-start.1
  28.6 14.2 %collective-permute-done.4 = bf16[192,768]{1,0:T(8,128)(2,1)S(1)} collective-permute-done((bf16[192,768]{1,0:T(8,128)(2,1)}, bf16[192,768]{1,0:T(8,128)(2,1)S(1)}, u32[]{:S(2)}, u32[]{:S(2)}) %collective-permute-start.4) | collective-permute-done | bytes 294944 | tf_op jit(solution)/shard_map/ppermute | solution.py:56
  45.8 1.6 fusion.190
  48.1 2.3 multiply_add_fusion
  50.4 3.0 multiply_convert_fusion.2
  57.4 1.7 collective-permute-start.12
  59.7 1.7 constant_dynamic-update-slice_fusion.7
  62.5 1.8 collective-permute-start.9
  65.4 7.7 %collective-permute-done.9 = f32[1,4]{1,0:T(1,128)S(1)} collective-permute-done((f32[1,4]{1,0:T(1,128)S(1)}, f32[1,4]{1,0:T(1,128)S(1)}, u32[]{:S(2)}, u32[]{:S(2)}) %collective-permute-start.9) | collective-permute-done | bytes 48 | tf_op jit(solution)/shard_map/ppermute | solution.py:56
  75.4 1.7 collective-permute-start.7
  77.9 1.7 constant_dynamic-update-slice_fusion.6
  79.6 1.7 constant_dynamic-update-slice_fusion.5
  82.1 4.5 collective-permute-done.7
  86.6 1.7 fusion.186
  91.5 1.7 fusion.137
  94.5 1.7 fusion.64
  97.7 1.8 fusion.91
  100.3 1.6 fusion.135
  103.5 1.7 fusion.65
  106.5 1.9 multiply_reduce_fusion.2
  110.9 1.7 collective-permute-start.18
  112.7 9.0 %collective-permute-done.18 = bf16[256,768]{1,0:T(8,128)(2,1)} collective-permute-done((bf16[256,768]{1,0:T(8,128)(2,1)}, bf16[256,768]{1,0:T(8,128)(2,1)}, u32[]{:S(2)}, u32[]{:S(2)}) %collective-permute-start.18) | collective-permute-done | bytes 393248 | tf_op jit(solution)/shard_map/ppermute | solution.py:56
  121.7 1.6 copy.34
  125.2 5.7 %convert_reduce_fusion = (f32[768]{0:T(1024)}, bf16[1024,768]{1,0:T(8,128)(2,1)S(1)}) fusion(f32[1024,768]{1,0:T(8,128)} %get-tuple-element.301, f32[768]{0:T(1024)S(1)} %copy-done.117, bf16[768,768]{1,0:T(8,128)(2,1)} %param.25, bf16[256,768]{1,0:T(8,128)(2,1)} %collective-permute-done.19, bf16[256,768]{1,0:T(8,128)(2,1)} %collective-permute-done.18, ...), kind=kOutput, calls=%fused_computation.54 | convolution fusion | flops 1226046720 | bytes 7477248 | tf_op jit(solution)/shard_map/dot_general | solution.py:38
  135.4 1.7 fusion.59
  137.1 2.0 pad_maximum_fusion
  140.4 1.8 collective-permute-start.21
  142.2 4.4 convolution_convert_fusion.5
  146.6 5.4 %collective-permute-done.21 = bf16[256,768]{1,0:T(8,128)(2,1)S(1)} collective-permute-done((bf16[256,768]{1,0:T(8,128)(2,1)S(1)}, bf16[256,768]{1,0:T(8,128)(2,1)S(1)}, u32[]{:S(2)}, u32[]{:S(2)}) %collective-permute-start.21) | collective-permute-done | bytes 393248 | tf_op jit(solution)/shard_map/ppermute | solution.py:56
  152.0 2.3 multiply_reduce_fusion.3
  156.8 1.8 collective-permute-start.22
  159.5 10.4 %collective-permute-done.22 = bf16[2,256,192]{2,1,0:T(8,128)(2,1)S(1)} collective-permute-done((bf16[2,256,192]{2,1,0:T(8,128)(2,1)S(1)}, bf16[2,256,192]{2,1,0:T(8,128)(2,1)S(1)}, u32[]{:S(2)}, u32[]{:S(2)}) %collective-permute-start.22) | collective-permute-done | bytes 196640 | tf_op jit(solution)/shard_map/ppermute | solution.py:56
  170.1 2.5 convolution_convert_fusion.6
  173.3 1.8 fusion.113
  175.1 2.5 collective-permute-start.27
  177.5 27.4 %while.28 = (s32[]{:T(128)}, f32[1024,3,64]{0,2,1:T(8,128)}, f32[1024,3,64]{0,2,1:T(8,128)}, bf16[2,512,3,64]{1,3,2,0:T(8,128)(2,1)}, bf16[2,512,3,64]{1,3,2,0:T...) while((s32[]{:T(128)}, f32[1024,3,64]{0,2,1:T(8,128)}, ...), condition=%wide.region_25.26_spmd.clone, body=%wide.region_23.25_spmd.clone.sunk | while | flops 1031305728 | bytes 112558992 | solution.py:145
  178.8 2.1 multiply_reduce_fusion.15
  181.5 1.7 multiply_convert_fusion.5
  183.2 2.6 fusion.255
  185.8 1.8 fusion.257
  187.6 3.4 fusion.256
  192.2 2.1 multiply_reduce_fusion.15
  194.8 1.7 multiply_convert_fusion.5
  196.5 2.9 fusion.255
  199.5 1.8 fusion.257
  201.2 3.7 fusion.256
  209.2 2.0 fusion.60
  211.2 2.0 fusion.115
  216.3 2.1 collective-permute-done.24
  218.7 11.1 %collective-permute-done.25 = bf16[256,768]{1,0:T(8,128)(2,1)S(1)} collective-permute-done((bf16[256,768]{1,0:T(8,128)(2,1)S(1)}, bf16[256,768]{1,0:T(8,128)(2,1)S(1)}, u32[]{:S(2)}, u32[]{:S(2)}) %collective-permute-start.25) | collective-permute-done | bytes 393248 | tf_op jit(solution)/shard_map/ppermute | solution.py:56
  230.8 146.3 %all-reduce.5.cloned.1.call-done = (bf16[3,768,192]{1,2,0:T(8,128)(2,1)}, bf16[192,768]{1,0:T(8,128)(2,1)}, bf16[768,768]{1,0:T(8,128)(2,1)}, bf16[768,768]{1,0:T(8,128)(2,1)}, bf16[576,768]{1,0:T(8,128)(2,1)}) async-done(((bf16[3,768,192]{1,2,0:T(8,128)(2,1)}, bf16[192,768]{1,0:T(8,128)(2,1)}, bf16[768,768]{1,0:T(8,128)(2,1)}, bf16[768,768]{1,0:T(8,128)(2,1)}, bf16[576,768]{1,0:T(8,128)(2,1)}), ...) | async-done | bytes 4423696 | tf_op jit(solution)/shard_map/psum | solution.py:325
  377.4 20.8 %all-reduce.1 = (f32[768]{0:T(1024)}, f32[]{:T(128)}) all-reduce(f32[768]{0:T(1024)S(1)} %copy-done.110, f32[]{:T(128)} %bitcast.73), channel_id=1, replica_groups=mesh['tok'=8,'ad'=4] {'tok'}, use_global_device_ids=true, to_apply=%region_30.31 | all-reduce | flops 769 | bytes 6152 | tf_op jit(solution)/shard_map/psum | solution.py:343
  398.3 37.4 %all-reduce = (f32[7,768]{1,0:T(8,128)S(1)}, f32[16]{0:T(128)S(1)}) all-reduce(f32[7,768]{1,0:T(8,128)S(1)} %stack.100, f32[16]{0:T(128)S(1)} %pad_maximum_fusion.34), channel_id=1, replica_groups=mesh['tok'=8,'ad'=4] {'tok','ad'}, use_global_device_ids=true, to_apply=%region_39.40 | all-reduce | flops 5392 | bytes 43136 | tf_op jit(solution)/shard_map/psum | solution.py:342
  438.2 3.4 convert_element_type.363
  441.6 1.6 convert_element_type.379
  443.3 1.6 convert_element_type.382
  447.1 4.9 %all-gather.8.cloned.1.call-done = bf16[2304,768]{1,0:T(8,128)(2,1)} async-done(((bf16[576,768]{1,0:T(8,128)(2,1)}), bf16[2304,768]{1,0:T(8,128)(2,1)}) %all-gather.8.cloned.1.call-update) | async-done | bytes 3538960 | tf_op jit(solution)/shard_map/all_gather | solution.py:322
  452.0 5.7 %convert.47 = f32[3,768,768]{2,1,0:T(8,128)} convert(bf16[3,768,768]{2,1,0:T(8,128)(2,1)} %bitcast.302) | non-fusion elementwise | flops 1769472 | bytes 10616832 | tf_op jit(solution)/shard_map/convert_element_type | solution.py:323
  (456 shorter events, 64.4 us)
Async XLA Ops:
  7.2 43.2 %copy-start = (bf16[768,768]{1,0:T(8,128)(2,1)S(1)}, bf16[768,768]{1,0:T(8,128)(2,1)}, u32[]{:S(2)}) copy-start(bf16[768,768]{1,0:T(8,128)(2,1)} %param.23) | copy-start | bytes 3538948
  7.2 206.0 %reduce-scatter.2.cloned.1.call-start = ((), (), s32[]{:S(2)}) async-start(), calls=%async_computation.3 | async-start | bytes 4423680 | tf_op jit(solution)/shard_map/reduce_scatter | solution.py:285
  11.4 15.5 %copy-start.108 = (f32[3,768]{1,0:T(4,128)S(1)}, f32[3,768]{1,0:T(4,128)}, u32[]{:S(2)}) copy-start(f32[3,768]{1,0:T(4,128)} %param.27) | copy-start | bytes 27652
  11.5 15.5 %copy-start.109 = (f32[3,768]{1,0:T(4,128)S(1)}, f32[3,768]{1,0:T(4,128)}, u32[]{:S(2)}) copy-start(f32[3,768]{1,0:T(4,128)} %param.28) | copy-start | bytes 27652
  23.7 19.2 %collective-permute-start = (bf16[1024,192]{0,1:T(8,128)(2,1)S(1)}, bf16[1024,192]{0,1:T(8,128)(2,1)S(1)}, u32[]{:S(2)}, u32[]{:S(2)}) collective-permute-start(bf16[1024,192]{0,1:T(8,128)(2,1)S(1)} %bitcast.306), channel_id=1, source_target_pairs={{0,1},{1,0},{2,3},{3,2},{4,5},{5,4},{6,7},{7,6},{8,9},{9,8},{10,11... | collective-permute-start | bytes 1179656 | tf_op jit(solution)/shard_map/ppermute | solution.py:56
  24.2 18.9 %collective-permute-start.1 = (bf16[1024,192]{0,1:T(8,128)(2,1)S(1)}, bf16[1024,192]{0,1:T(8,128)(2,1)S(1)}, u32[]{:S(2)}, u32[]{:S(2)}) collective-permute-start(bf16[1024,192]{0,1:T(8,128)(2,1)S(1)} %bitcast.307), channel_id=1, source_target_pairs={{0,2},{1,3},{2,0},{3,1},{4,6},{5,7},{6,4},{7,5},{8,10},{9,11},{10,... | collective-permute-start | bytes 1179656 | tf_op jit(solution)/shard_map/ppermute | solution.py:56
  26.8 16.0 %collective-permute-start.4 = (bf16[192,768]{1,0:T(8,128)(2,1)}, bf16[192,768]{1,0:T(8,128)(2,1)S(1)}, u32[]{:S(2)}, u32[]{:S(2)}) collective-permute-start(bf16[192,768]{1,0:T(8,128)(2,1)} %param.22), channel_id=1, source_target_pairs={{0,2},{1,3},{2,0},{3,1},{4,6},{5,7},{6,4},{7,5},{8,10},{9,11},{10,... | collective-permute-start | bytes 884744 | tf_op jit(solution)/shard_map/ppermute | solution.py:56
  26.9 15.9 %collective-permute-start.3 = (bf16[192,768]{1,0:T(8,128)(2,1)}, bf16[192,768]{1,0:T(8,128)(2,1)S(1)}, u32[]{:S(2)}, u32[]{:S(2)}) collective-permute-start(bf16[192,768]{1,0:T(8,128)(2,1)} %param.22), channel_id=1, source_target_pairs={{0,1},{1,0},{2,3},{3,2},{4,5},{5,4},{6,7},{7,6},{8,9},{9,8},{10,11... | collective-permute-start | bytes 884744 | tf_op jit(solution)/shard_map/ppermute | solution.py:56
  27.0 21.1 %copy-start.84 = (f32[768]{0:T(1024)}, f32[768]{0:T(1024)S(1)}, u32[]{:S(2)}) copy-start(f32[768]{0:T(1024)S(1)} %get-tuple-element.191) | copy-start | bytes 9220
  42.8 1.6 collective-permute-start.5
  43.1 1.9 collective-permute-start.2
  57.0 5.5 %collective-permute-start.6 = (bf16[2,256,768]{2,1,0:T(8,128)(2,1)}, bf16[2,256,768]{2,1,0:T(8,128)(2,1)S(1)}, u32[]{:S(2)}, u32[]{:S(2)}) collective-permute-start(bf16[2,256,768]{2,1,0:T(8,128)(2,1)} %pad_maximum_fusion.5), channel_id=1, source_target_pairs={{0,1},{1,0},{2,3},{3,2},{4,5},{5,4},{6,7},{7,6},{8,9},{9,8},{10,11... | collective-permute-start | bytes 2359304 | tf_op jit(solution)/shard_map/ppermute | solution.py:56
  57.4 17.0 %collective-permute-start.12 = (bf16[768,192]{0,1:T(8,128)(2,1)}, bf16[768,192]{0,1:T(8,128)(2,1)}, u32[]{:S(2)}, u32[]{:S(2)}) collective-permute-start(bf16[768,192]{0,1:T(8,128)(2,1)} %param.29), channel_id=1, source_target_pairs={{0,2},{1,3},{2,0},{3,1},{4,6},{5,7},{6,4},{7,5},{8,10},{9,11},{10,... | collective-permute-start | bytes 884744 | tf_op jit(solution)/shard_map/ppermute | solution.py:56
  59.2 18.7 %collective-permute-start.11 = (bf16[768,192]{0,1:T(8,128)(2,1)}, bf16[768,192]{0,1:T(8,128)(2,1)}, u32[]{:S(2)}, u32[]{:S(2)}) collective-permute-start(bf16[768,192]{0,1:T(8,128)(2,1)} %param.29), channel_id=1, source_target_pairs={{0,1},{1,0},{2,3},{3,2},{4,5},{5,4},{6,7},{7,6},{8,9},{9,8},{10,11... | collective-permute-start | bytes 884744 | tf_op jit(solution)/shard_map/ppermute | solution.py:56
  59.2 18.7 %collective-permute-start.15 = (bf16[192,768]{1,0:T(8,128)(2,1)}, bf16[192,768]{1,0:T(8,128)(2,1)}, u32[]{:S(2)}, u32[]{:S(2)}) collective-permute-start(bf16[192,768]{1,0:T(8,128)(2,1)} %bitcast.38), channel_id=1, source_target_pairs={{0,2},{1,3},{2,0},{3,1},{4,6},{5,7},{6,4},{7,5},{8,10},{9,11},{10,... | collective-permute-start | bytes 884744 | tf_op jit(solution)/shard_map/ppermute | solution.py:56
  59.5 32.0 %collective-permute-start.14 = (bf16[192,768]{1,0:T(8,128)(2,1)}, bf16[192,768]{1,0:T(8,128)(2,1)}, u32[]{:S(2)}, u32[]{:S(2)}) collective-permute-start(bf16[192,768]{1,0:T(8,128)(2,1)} %bitcast.38), channel_id=1, source_target_pairs={{0,1},{1,0},{2,3},{3,2},{4,5},{5,4},{6,7},{7,6},{8,9},{9,8},{10,11... | collective-permute-start | bytes 884744 | tf_op jit(solution)/shard_map/ppermute | solution.py:56
  62.5 19.6 %copy-start.35 = (bf16[2,256,768]{2,1,0:T(8,128)(2,1)}, bf16[2,256,768]{2,1,0:T(8,128)(2,1)S(1)}, u32[]{:S(2)}) copy-start(bf16[2,256,768]{2,1,0:T(8,128)(2,1)S(1)} %collective-permute-done.6) | copy-start | bytes 2359300
  62.5 10.6 %collective-permute-start.9 = (f32[1,4]{1,0:T(1,128)S(1)}, f32[1,4]{1,0:T(1,128)S(1)}, u32[]{:S(2)}, u32[]{:S(2)}) collective-permute-start(f32[1,4]{1,0:T(1,128)S(1)} %get-tuple-element.297), channel_id=1, source_target_pairs={{0,2},{1,3},{2,0},{3,1},{4,6},{5,7},{6,4},{7,5},{8,10},{9,11},{10,... | collective-permute-start | bytes 56 | tf_op jit(solution)/shard_map/ppermute | solution.py:56
  73.1 1.1 collective-permute-start.8
  74.2 1.1 collective-permute-start.10
  74.4 6.9 %collective-permute-start.13 = (bf16[768,192]{0,1:T(8,128)(2,1)}, bf16[768,192]{0,1:T(8,128)(2,1)S(1)}, u32[]{:S(2)}, u32[]{:S(2)}) collective-permute-start(bf16[768,192]{0,1:T(8,128)(2,1)} %collective-permute-done.12), channel_id=1, source_target_pairs={{0,1},{1,0},{2,3},{3,2},{4,5},{5,4},{6,7},{7,6},{8,9},{9,8},{10,11... | collective-permute-start | bytes 884744 | tf_op jit(solution)/shard_map/ppermute | solution.py:56
  75.4 11.2 %collective-permute-start.7 = (bf16[256,768]{1,0:T(8,128)(2,1)S(1)}, bf16[256,768]{1,0:T(8,128)(2,1)S(1)}, u32[]{:S(2)}, u32[]{:S(2)}) collective-permute-start(bf16[256,768]{1,0:T(8,128)(2,1)S(1)} %fusion.107), channel_id=1, source_target_pairs={{0,2},{1,3},{2,0},{3,1},{4,6},{5,7},{6,4},{7,5},{8,10},{9,11},{10,... | collective-permute-start | bytes 1179656 | tf_op jit(solution)/shard_map/ppermute | solution.py:56
  77.8 13.6 %collective-permute-start.16 = (bf16[192,768]{1,0:T(8,128)(2,1)}, bf16[192,768]{1,0:T(8,128)(2,1)S(1)}, u32[]{:S(2)}, u32[]{:S(2)}) collective-permute-start(bf16[192,768]{1,0:T(8,128)(2,1)} %collective-permute-done.15), channel_id=1, source_target_pairs={{0,1},{1,0},{2,3},{3,2},{4,5},{5,4},{6,7},{7,6},{8,9},{9,8},{10,11... | collective-permute-start | bytes 884744 | tf_op jit(solution)/shard_map/ppermute | solution.py:56
  79.6 8.9 %copy-start.98 = (f32[768]{0:T(1024)S(1)}, f32[768]{0:T(1024)}, u32[]{:S(2)}) copy-start(f32[768]{0:T(1024)} %get-tuple-element.195) | copy-start | bytes 9220
  88.3 20.1 %copy-start.86 = (f32[256]{0:T(256)}, f32[256]{0:T(256)S(1)}, u32[]{:S(2)}) copy-start(f32[256]{0:T(256)S(1)} %broadcast_multiply_fusion.8) | copy-start | bytes 3076
  88.5 19.8 %copy-start.93 = (f32[256]{0:T(256)}, f32[256]{0:T(256)S(1)}, u32[]{:S(2)}) copy-start(f32[256]{0:T(256)S(1)} %add_rsqrt_fusion.2) | copy-start | bytes 3076
  96.8 9.4 %copy-start.8 = (f32[256,768]{1,0:T(8,128)}, f32[256,768]{1,0:T(8,128)S(1)}, u32[]{:S(2)}) copy-start(f32[256,768]{1,0:T(8,128)S(1)} %get-tuple-element.309) | copy-start | bytes 2359300
  96.8 9.4 %copy-start.88 = (f32[256]{0:T(256)}, f32[256]{0:T(256)S(1)}, u32[]{:S(2)}) copy-start(f32[256]{0:T(256)S(1)} %broadcast_multiply_fusion.7) | copy-start | bytes 3076
  97.1 9.2 %copy-start.101 = (f32[256]{0:T(256)}, f32[256]{0:T(256)S(1)}, u32[]{:S(2)}) copy-start(f32[256]{0:T(256)S(1)} %add_rsqrt_fusion.1) | copy-start | bytes 3076
  99.5 6.8 %copy-start.106 = (f32[256]{0:T(256)}, f32[256]{0:T(256)S(1)}, u32[]{:S(2)}) copy-start(f32[256]{0:T(256)S(1)} %broadcast_multiply_fusion.6) | copy-start | bytes 3076
  108.3 13.3 %copy-start.26 = (bf16[2,512,192]{1,2,0:T(8,128)(2,1)S(1)}, bf16[2,512,192]{1,2,0:T(8,128)(2,1)}, u32[]{:S(2)}) copy-start(bf16[2,512,192]{1,2,0:T(8,128)(2,1)} %get-tuple-element.104) | copy-start | bytes 1179652
  109.3 15.9 %copy-start.117 = (f32[768]{0:T(1024)S(1)}, f32[768]{0:T(1024)}, u32[]{:S(2)}) copy-start(f32[768]{0:T(1024)} %param.24) | copy-start | bytes 9220
  110.9 10.7 %collective-permute-start.18 = (bf16[256,768]{1,0:T(8,128)(2,1)}, bf16[256,768]{1,0:T(8,128)(2,1)}, u32[]{:S(2)}, u32[]{:S(2)}) collective-permute-start(bf16[256,768]{1,0:T(8,128)(2,1)} %convert_element_type.338), channel_id=1, source_target_pairs={{0,2},{1,3},{2,0},{3,1},{4,6},{5,7},{6,4},{7,5},{8,10},{9,11},{10,... | collective-permute-start | bytes 1179656 | tf_op jit(solution)/shard_map/ppermute | solution.py:56
  112.7 12.5 %collective-permute-start.17 = (bf16[256,768]{1,0:T(8,128)(2,1)}, bf16[256,768]{1,0:T(8,128)(2,1)}, u32[]{:S(2)}, u32[]{:S(2)}) collective-permute-start(bf16[256,768]{1,0:T(8,128)(2,1)} %convert_element_type.338), channel_id=1, source_target_pairs={{0,1},{1,0},{2,3},{3,2},{4,5},{5,4},{6,7},{7,6},{8,9},{9,8},{10,11... | collective-permute-start | bytes 1179656 | tf_op jit(solution)/shard_map/ppermute | solution.py:56
  121.7 3.5 collective-permute-start.19
  133.5 5.6 %collective-permute-start.20 = (bf16[2,256,768]{2,1,0:T(8,128)(2,1)S(1)}, bf16[2,256,768]{2,1,0:T(8,128)(2,1)}, u32[]{:S(2)}, u32[]{:S(2)}) collective-permute-start(bf16[2,256,768]{2,1,0:T(8,128)(2,1)S(1)} %pad_maximum_fusion.6), channel_id=1, source_target_pairs={{0,1},{1,0},{2,3},{3,2},{4,5},{5,4},{6,7},{7,6},{8,9},{9,8},{10,11... | collective-permute-start | bytes 2359304 | tf_op jit(solution)/shard_map/ppermute | solution.py:56
  139.1 238.0 %all-reduce.5.cloned.1.call-start = ((), (), s32[]{:S(2)}) async-start(), calls=%async_computation.5 | async-start | bytes 8847360 | tf_op jit(solution)/shard_map/psum | solution.py:325
  140.4 11.6 %copy-start.12 = (f32[1024,768]{1,0:T(8,128)S(1)}, f32[1024,768]{1,0:T(8,128)}, u32[]{:S(2)}) copy-start(f32[1024,768]{1,0:T(8,128)} %get-tuple-element.249) | copy-start | bytes 9437188
  140.4 11.6 %copy-start.14 = (f32[256,768]{1,0:T(8,128)S(1)}, f32[256,768]{1,0:T(8,128)}, u32[]{:S(2)}) copy-start(f32[256,768]{1,0:T(8,128)} %copy-done.13) | copy-start | bytes 2359300
  140.4 11.5 %copy-start.85 = (f32[768]{0:T(1024)S(1)}, f32[768]{0:T(1024)}, u32[]{:S(2)}) copy-start(f32[768]{0:T(1024)} %copy-done.84) | copy-start | bytes 9220
  140.4 11.5 %collective-permute-start.21 = (bf16[256,768]{1,0:T(8,128)(2,1)S(1)}, bf16[256,768]{1,0:T(8,128)(2,1)S(1)}, u32[]{:S(2)}, u32[]{:S(2)}) collective-permute-start(bf16[256,768]{1,0:T(8,128)(2,1)S(1)} %fusion.104), channel_id=1, source_target_pairs={{0,2},{1,3},{2,0},{3,1},{4,6},{5,7},{6,4},{7,5},{8,10},{9,11},{10,... | collective-permute-start | bytes 1179656 | tf_op jit(solution)/shard_map/ppermute | solution.py:56
  146.6 7.7 %slice-start = ((f32[1024]{0:T(1024)}), f32[256]{0:T(256)S(1)}, s32[]{:S(2)}) async-start(f32[1024]{0:T(1024)} %copy-done.90), calls=%async_computation.6 | async-start | bytes 2048 | tf_op jit(solution)/shard_map/slice | solution.py:301
  156.6 16.7 %copy-start.32 = (bf16[768,768]{1,0:T(8,128)(2,1)}, bf16[768,768]{1,0:T(8,128)(2,1)S(1)}, u32[]{:S(2)}) copy-start(bf16[768,768]{1,0:T(8,128)(2,1)S(1)} %convolution_convert_fusion.7) | copy-start | bytes 3538948
  156.6 13.5 %copy-start.16 = (f32[1024,768]{1,0:T(8,128)S(1)}, f32[1024,768]{1,0:T(8,128)}, u32[]{:S(2)}) copy-start(f32[1024,768]{1,0:T(8,128)} %copy-done.15) | copy-start | bytes 9437188
  156.6 13.5 %copy-start.120 = (bf16[1024,768]{1,0:T(8,128)(2,1)S(1)}, bf16[1024,768]{1,0:T(8,128)(2,1)}, u32[]{:S(2)}) copy-start(bf16[1024,768]{1,0:T(8,128)(2,1)} %copy-done.119) | copy-start | bytes 4718596
  156.8 13.1 %collective-permute-start.22 = (bf16[2,256,192]{2,1,0:T(8,128)(2,1)S(1)}, bf16[2,256,192]{2,1,0:T(8,128)(2,1)S(1)}, u32[]{:S(2)}, u32[]{:S(2)}) collective-permute-start(bf16[2,256,192]{2,1,0:T(8,128)(2,1)S(1)} %pad_maximum_fusion.32), channel_id=1, source_target_pairs={{0,2},{1,3},{2,0},{3,1},{4,6},{5,7},{6,4},{7,5},{8,10},{9,11},{10,... | collective-permute-start | bytes 589832 | tf_op jit(solution)/shard_map/ppermute | solution.py:56
  159.5 13.8 %collective-permute-start.26 = (bf16[2,192,768]{2,1,0:T(8,128)(2,1)}, bf16[2,192,768]{2,1,0:T(8,128)(2,1)}, u32[]{:S(2)}, u32[]{:S(2)}) collective-permute-start(bf16[2,192,768]{2,1,0:T(8,128)(2,1)} %pad_maximum_fusion.8), channel_id=1, source_target_pairs={{0,1},{1,0},{2,3},{3,2},{4,5},{5,4},{6,7},{7,6},{8,9},{9,8},{10,11... | collective-permute-start | bytes 1769480 | tf_op jit(solution)/shard_map/ppermute | solution.py:56
  170.0 2.6 collective-permute-start.23
  175.1 36.2 %collective-permute-start.27 = (bf16[192,768]{1,0:T(8,128)(2,1)}, bf16[192,768]{1,0:T(8,128)(2,1)}, u32[]{:S(2)}, u32[]{:S(2)}) collective-permute-start(bf16[192,768]{1,0:T(8,128)(2,1)} %fusion.113), channel_id=1, source_target_pairs={{0,2},{1,3},{2,0},{3,1},{4,6},{5,7},{6,4},{7,5},{8,10},{9,11},{10,... | collective-permute-start | bytes 884744 | tf_op jit(solution)/shard_map/ppermute | solution.py:56
  213.2 224.9 %all-gather.4.cloned.1.call-start = ((), (), s32[]{:S(2)}) async-start(), calls=%async_computation.1 | async-start | bytes 1966080 | tf_op jit(solution)/shard_map/all_gather | solution.py:284
  214.0 224.2 %all-gather.6.cloned.1.call-start = ((), (), s32[]{:S(2)}) async-start(), calls=%async_computation.2 | async-start | bytes 1966080 | tf_op jit(solution)/shard_map/all_gather | solution.py:320
  215.8 14.0 %copy-start.11 = (f32[256,768]{1,0:T(8,128)S(1)}, f32[256,768]{1,0:T(8,128)}, u32[]{:S(2)}) copy-start(f32[256,768]{1,0:T(8,128)} %copy-done.10) | copy-start | bytes 2359300
  216.0 161.2 %copy-start.111 = (f32[16]{0:T(128)S(1)}, f32[16]{0:T(128)}, u32[]{:S(2)}) copy-start(f32[16]{0:T(128)} %get-tuple-element.188) | copy-start | bytes 196
  216.0 161.3 %copy-start.97 = (f32[768]{0:T(1024)S(1)}, f32[768]{0:T(1024)}, u32[]{:S(2)}) copy-start(f32[768]{0:T(1024)} %get-tuple-element.239) | copy-start | bytes 9220
  216.0 161.3 %copy-start.92 = (f32[768]{0:T(1024)S(1)}, f32[768]{0:T(1024)}, u32[]{:S(2)}) copy-start(f32[768]{0:T(1024)} %get-tuple-element.181) | copy-start | bytes 9220
  216.0 161.3 %copy-start.91 = (f32[768]{0:T(1024)S(1)}, f32[768]{0:T(1024)}, u32[]{:S(2)}) copy-start(f32[768]{0:T(1024)} %get-tuple-element.186) | copy-start | bytes 9220
  216.0 161.3 %copy-start.96 = (f32[768]{0:T(1024)S(1)}, f32[768]{0:T(1024)}, u32[]{:S(2)}) copy-start(f32[768]{0:T(1024)} %get-tuple-element.178) | copy-start | bytes 9220
  216.0 161.3 %copy-start.95 = (f32[768]{0:T(1024)S(1)}, f32[768]{0:T(1024)}, u32[]{:S(2)}) copy-start(f32[768]{0:T(1024)} %get-tuple-element.183) | copy-start | bytes 9220
  216.0 161.4 %copy-start.110 = (f32[768]{0:T(1024)S(1)}, f32[768]{0:T(1024)}, u32[]{:S(2)}) copy-start(f32[768]{0:T(1024)} %get-tuple-element.314) | copy-start | bytes 9220
  216.0 182.2 %copy-start.103 = (f32[768]{0:T(1024)S(1)}, f32[768]{0:T(1024)}, u32[]{:S(2)}) copy-start(f32[768]{0:T(1024)} %get-tuple-element.176) | copy-start | bytes 9220
  216.0 2.4 collective-permute-start.24
  218.5 11.3 %collective-permute-start.25 = (bf16[256,768]{1,0:T(8,128)(2,1)S(1)}, bf16[256,768]{1,0:T(8,128)(2,1)S(1)}, u32[]{:S(2)}, u32[]{:S(2)}) collective-permute-start(bf16[256,768]{1,0:T(8,128)(2,1)S(1)} %fusion.100), channel_id=1, source_target_pairs={{0,2},{1,3},{2,0},{3,1},{4,6},{5,7},{6,4},{7,5},{8,10},{9,11},{10,... | collective-permute-start | bytes 1179656 | tf_op jit(solution)/shard_map/ppermute | solution.py:56
  230.8 221.2 %all-gather.8.cloned.1.call-start = ((), (), s32[]{:S(2)}) async-start(), calls=%async_computation.4 | async-start | bytes 4423680 | tf_op jit(solution)/shard_map/all_gather | solution.py:322
  452.0 6.9 %copy-start.1 = (bf16[768,768]{1,0:T(8,128)(2,1)S(1)}, bf16[768,768]{1,0:T(8,128)(2,1)}, u32[]{:S(2)}) copy-start(bf16[768,768]{1,0:T(8,128)(2,1)} %param.23) | copy-start | bytes 3538948
  (105 other events, 237.1 us)
Sparse Core Ops, SparseCore 0:
  139.2 50.3 reduce-scatter.1
  213.3 163.7 all-reduce.4
  378.8 18.4 all-gather.3
  399.4 19.8 all-gather.5
  420.7 31.1 all-gather.7
